TPU v7x, 128 devices: a whole 4x4x4 slice. The times are simulated.
128 devices in a mesh: shard: 128 (over x, y, z, core).
Axes of the slice: x: 4, y: 4, z: 4, core: 2. Of those that a mesh axis runs over, the one named last changes fastest.
Arguments:
- embeddings: bfloat16 [262144, 1024], P('shard'), may hold values from -6 to 6
- block_rows: int32 [2048], P('shard'), may hold values from 1 to 128, 196608 in all
- pairs: int32 [65536, 3], P('shard'), may hold values from 0 to 2047, as said below
Outputs:
- best: float32 [2048, 128], P('shard')
Inputs may be any that keep to these rules, and one draw needn't show every extreme that they name: `pairs`: entries d * 512 to (d + 1) * 512 - 1 are device d's. Each is (row block, column block, scorer); the scorer is d for a live entry and 128 for an unused one. The column block is always one of device d's blocks; the row block is one of device d's or of another device. Exactly 64 entries of device d have a row block of another device, all live, each from a different device; and the blocks of each device are row blocks of such entries of exactly 64 other devices. Live entries of one device number 64 to 512, and some device has 512.
All inputs are finite; a program needn't handle non-finite values. No bound on the sum of `block_rows` on one device may be relied on, other than what follows from the above.
Results may differ from a plain program's by a relative error of at most 0.0003.
Values may be sent and summed in bfloat16 or wider, within the bound.
No kernel may reach another device: no remote copies, remote signals or barrier semaphores. Data moves between devices by JAX's collectives and lax.ppermute only.
A program may use at most 256 MiB of HBM per device.

v0:
```python
import jax
import jax.numpy as jnp
from jax import lax
from jax.sharding import PartitionSpec as P


def normalize(embeddings, blocks):
    values = embeddings.astype(jnp.float32)
    scaled = values * lax.rsqrt(jnp.sum(values * values, axis=-1, keepdims=True) + 1e-06)
    return scaled.astype(jnp.bfloat16).reshape(blocks, -1, values.shape[1])


def one_hot(index, count, valid):
    return (index[:, None] == jnp.arange(count, dtype=jnp.int32)[None, :]) & valid[:, None]


def select_tiles(selector, unit):
    blocks, width, depth = unit.shape
    picked = jnp.dot(
        selector.astype(jnp.bfloat16),
        unit.reshape(blocks, width * depth),
        preferred_element_type=jnp.bfloat16,
    )
    return picked.reshape(selector.shape[0], width, depth)


def select_counts(selector, block_rows):
    return jnp.sum(jnp.where(selector, block_rows[None, :], 0), axis=1)


def fold_maxima(selector, maxima):
    spread = jnp.where(selector[:, :, None], maxima[:, None, :], -1.0)
    return spread.max(axis=0)


def pair_maxima(rows, cols, row_count, col_count, valid):
    scores = jnp.einsum("pid,pjd->pij", rows, cols, preferred_element_type=jnp.float32)
    index = jnp.arange(rows.shape[1], dtype=jnp.int32)
    keep = (index[None, :, None] < row_count[:, None, None]) & (
        index[None, None, :] < col_count[:, None, None]
    )
    keep = keep & valid[:, None, None]
    masked = jnp.where(keep, scores, -1.0)
    return (masked.max(axis=2), masked.max(axis=1))


def local_maxima(unit, block_rows, linked):
    blocks, width, depth = unit.shape
    total = blocks * width
    flat = unit.reshape(total, depth)
    live_flat = (jnp.arange(width, dtype=jnp.int32)[None, :] < block_rows[:, None]).reshape(total)
    linked_rows = jnp.repeat(linked, width, axis=0)
    span = min(512, total)
    columns = jnp.arange(total, dtype=jnp.int32)

    def tile(number):
        start = number * span
        query = lax.dynamic_slice_in_dim(flat, start, span, 0)
        scores = lax.dot_general(
            query, flat, (((1,), (1,)), ((), ())), preferred_element_type=jnp.float32
        )
        ids = start + jnp.arange(span, dtype=jnp.int32)
        link = jnp.repeat(lax.dynamic_slice_in_dim(linked_rows, start, span, 0), width, axis=1)
        keep = (
            link & live_flat[None, :] & lax.dynamic_slice_in_dim(live_flat, start, span, 0)[:, None]
        )
        keep = keep & (ids[:, None] != columns[None, :])
        return jnp.where(keep, scores, -1.0).max(axis=1)

    result = lax.map(tile, jnp.arange(total // span, dtype=jnp.int32))
    return result.reshape(blocks, width)


def on_device(embeddings, block_rows, pairs):
    blocks = block_rows.shape[0]
    unit = normalize(embeddings, blocks)
    peers = lax.axis_size("shard")
    myself = lax.axis_index("shard")
    row_block = pairs[:, 0]
    col_block = pairs[:, 1]
    alive = pairs[:, 2] == myself
    owner = row_block // blocks
    remote = alive & (owner != myself)
    row_local = row_block % blocks
    col_local = col_block % blocks
    nearby = alive & ~remote
    row_table = one_hot(row_local, blocks, nearby).astype(jnp.float32)
    col_table = one_hot(col_local, blocks, nearby).astype(jnp.float32)
    adjacency = (
        lax.dot_general(
            row_table, col_table, (((0,), (0,)), ((), ())), preferred_element_type=jnp.float32
        )
        > 0.5
    )
    linked = adjacency | adjacency.T
    best = local_maxima(unit, block_rows, linked)
    request = (
        jnp.full((peers,), -1, jnp.int32)
        .at[jnp.where(remote, owner, peers)]
        .set(row_local, mode="drop")
    )
    wanted = lax.all_to_all(
        request.reshape(peers, 1), "shard", split_axis=0, concat_axis=0, tiled=True
    )[:, 0]
    present = wanted >= 0
    send_table = one_hot(wanted, blocks, present)
    outgoing = select_tiles(send_table, unit)
    out_rows = select_counts(send_table, block_rows).reshape(peers, 1)
    partner = (
        jnp.full((peers,), -1, jnp.int32)
        .at[jnp.where(remote, owner, peers)]
        .set(col_local, mode="drop")
    )
    partner_table = one_hot(partner, blocks, partner >= 0)
    partner_tiles = select_tiles(partner_table, unit)
    partner_rows = select_counts(partner_table, block_rows)
    arrived, arrived_rows = (
        lax.all_to_all(outgoing, "shard", split_axis=0, concat_axis=0, tiled=True),
        lax.all_to_all(out_rows, "shard", split_axis=0, concat_axis=0, tiled=True),
    )
    row_max, col_max = pair_maxima(
        arrived, partner_tiles, arrived_rows[:, 0], partner_rows, partner >= 0
    )
    best = jnp.maximum(best, fold_maxima(partner_table, col_max))
    returned = lax.all_to_all(row_max, "shard", split_axis=0, concat_axis=0, tiled=True)
    best = jnp.maximum(best, fold_maxima(send_table, returned))
    return best


def solution(mesh):
    placed = (P("shard", None), P("shard"), P("shard", None))
    return jax.shard_map(
        on_device, mesh=mesh, in_specs=placed, out_specs=P("shard", None), check_vma=False
    )
```

profile of v0, /device:TPU:1, one launch (start us, length us, event | category | flops | bytes accessed | tf_op | source)
XLA Modules:
  0.0 712.0 jit_solution(9729697531966671306)
XLA Ops:
  0.0 0.8 and_reduce_fusion
  0.8 0.8 and_select_fusion.1
  1.7 2.4 scatter_custom_fusion.1
  4.1 0.7 copy.35
  4.8 11.5 %all-to-all-start = ((s32[128,1,1]{2,1,0:T(1,128)}), s32[128,1,1]{2,1,0:T(1,128)S(1)}, u32[]{:S(2)}, u32[]{:S(2)}) async-start(s32[128,1,1]{2,1,0:T(1,128)} %copy.35), calls=%async_computation | async-start | bytes 131072 | tf_op jit(solution)/shard_map/all_to_all | solution.py:102
  16.3 3.1 fusion.11
  19.4 2.4 scatter_custom_fusion
  21.9 4.9 fusion.12
  26.8 4.8 reshape_reshape.4
  31.6 2.4 reduce.1
  34.1 0.7 copy.36
  34.8 9.8 %all-to-all-start.1 = ((s32[128,1,1]{2,1,0:T(1,128)}), s32[128,1,1]{2,1,0:T(1,128)S(1)}, u32[]{:S(2)}, u32[]{:S(2)}) async-start(s32[128,1,1]{2,1,0:T(1,128)} %copy.36), calls=%async_computation.1 | async-start | bytes 131072 | tf_op jit(solution)/shard_map/all_to_all | solution.py:119
  44.6 15.8 %fusion.17 = bf16[128,128,1024]{2,0,1:T(8,128)(2,1)} fusion(bf16[2,128,8,1024]{3,2,1,0:T(8,128)(2,1)} %bitcast.54, s32[128]{0:T(128)S(1)} %reduce.1, pred[128]{0:T(512)(128)(4,1)S(1)} %broadcast_compare_fusion), kind=kOutput, calls=%fused_computation.26 | convolution fusion | flops 536875008 | bytes 37749376 | tf_op jit(solution)/shard_map/dot_general | solution.py:19
  60.4 30.7 %copy.38 = bf16[128,128,1024]{2,1,0:T(8,128)(2,1)} copy(bf16[128,128,1024]{2,0,1:T(8,128)(2,1)} %fusion.17) | data formatting | bytes 67108864 | tf_op jit(solution)/shard_map/dot_general | solution.py:19
  91.1 10.2 %all-to-all-start.2 = ((bf16[128,128,1024]{2,1,0:T(8,128)(2,1)}), bf16[128,128,1024]{2,1,0:T(8,128)(2,1)}, u32[]{:S(2)}, u32[]{:S(2)}) async-start(bf16[128,128,1024]{2,1,0:T(8,128)(2,1)} %copy.38), calls=%async_computation.2 | async-start | bytes 67108864 | tf_op jit(solution)/shard_map/all_to_all | solution.py:118
  102.3 42.0 %while.11 = (s32[]{:T(128)}, f32[4,512]{1,0:T(4,128)S(1)}, s32[4]{0:T(128)S(1)}, pred[2048,16]{1,0:T(8,128)(4,1)S(1)}, pred[2048]{0:T(1024)(128)(4,1)S(1)}, /*in...) while((s32[]{:T(128)}, f32[4,512]{1,0:T(4,128)S(1)}, ...), condition=%wide.region_3.4_spmd.clone, body=%wide.region_1.3_spmd.clone.sunk | while | flops 2153777152 | bytes 7380739 | solution.py:70
  102.3 0.7 dynamic_slice.26
  103.8 3.5 broadcast_in_dim.136
  107.3 5.5 select_reduce_fusion.6
  114.3 3.5 broadcast_in_dim.136
  117.8 5.5 select_reduce_fusion.6
  124.8 3.5 broadcast_in_dim.136
  128.3 5.5 select_reduce_fusion.6
  133.8 0.7 dynamic_slice.26
  135.3 3.5 broadcast_in_dim.136
  138.8 5.5 select_reduce_fusion.6
  144.3 15.9 %fusion.15 = bf16[128,128,1024]{2,0,1:T(8,128)(2,1)} fusion(bf16[2,128,8,1024]{3,2,1,0:T(8,128)(2,1)} %bitcast.55, s32[128]{0:T(128)S(1)} %scatter_custom_fusion, pred[128]{0:T(512)(128)(4,1)S(1)} %broadcast_compare_fusion.1), kind=kOutput, calls=%fused_computation.24 | convolution fusion | flops 536875008 | bytes 37749376 | tf_op jit(solution)/shard_map/dot_general | solution.py:19
  160.5 2.4 reduce.2
  162.9 454.8 %all-to-all-done.2 = bf16[128,128,1024]{2,1,0:T(8,128)(2,1)} async-done(((bf16[128,128,1024]{2,1,0:T(8,128)(2,1)}), bf16[128,128,1024]{2,1,0:T(8,128)(2,1)}, u32[]{:S(2)}, u32[]{:S(2)}) %all-to-all-start.2) | async-done | bytes 33554464 | tf_op jit(solution)/shard_map/all_to_all | solution.py:118
  617.8 40.5 %fusion.14 = (f32[128,128]{1,0:T(8,128)S(1)}, f32[128,128]{1,0:T(8,128)}) fusion(pred[128]{0:T(512)(128)(4,1)S(1)} %broadcast_compare_fusion.1, pred[128,128]{1,0:T(8,128)(4,1)S(1)} %iota_compare_fusion.4, pred[128,128]{1,0:T(8,128)(4,1)S(1)} %iota_compare_fusion.5, bf16[128,128,1024]{2,1,0:T(8,128)(2,1)} %all-to-all-done.2, bf16[128,128,1024]{2,0,1:T(8,128)(2,1)} %fusion.15), kind=kOutput, calls=%fused_computation.23 | convolution fusion | flops 4305420288 | bytes 67272832 | tf_op jit(solution)/shard_map/pid,pjd->pij/dot_general | solution.py:37
  658.2 43.4 %all-to-all-start.3 = ((f32[128,1,128]{2,1,0:T(1,128)}), f32[128,1,128]{2,1,0:T(1,128)S(1)}, u32[]{:S(2)}, u32[]{:S(2)}) async-start(f32[128,1,128]{2,1,0:T(1,128)} %bitcast.13), calls=%async_computation.3 | async-start | bytes 131072 | tf_op jit(solution)/shard_map/all_to_all | solution.py:125
  702.0 9.0 %all-to-all-done.3 = f32[128,1,128]{2,1,0:T(1,128)S(1)} async-done(((f32[128,1,128]{2,1,0:T(1,128)}), f32[128,1,128]{2,1,0:T(1,128)S(1)}, u32[]{:S(2)}, u32[]{:S(2)}) %all-to-all-start.3) | async-done | bytes 65568 | tf_op jit(solution)/shard_map/all_to_all | solution.py:125
  (49 shorter events, 4.8 us)
Async XLA Ops:
  4.8 26.8 %all-to-all-start = ((s32[128,1,1]{2,1,0:T(1,128)}), s32[128,1,1]{2,1,0:T(1,128)S(1)}, u32[]{:S(2)}, u32[]{:S(2)}) async-start(s32[128,1,1]{2,1,0:T(1,128)} %copy.35), calls=%async_computation | async-start | bytes 131072 | tf_op jit(solution)/shard_map/all_to_all | solution.py:102
  26.8 7.2 %copy-start = (s32[16]{0:T(128)S(1)}, s32[16]{0:T(128)}, u32[]{:S(2)}) copy-start(s32[16]{0:T(128)} %param.6) | copy-start | bytes 196
  34.8 56.3 %all-to-all-start.1 = ((s32[128,1,1]{2,1,0:T(1,128)}), s32[128,1,1]{2,1,0:T(1,128)S(1)}, u32[]{:S(2)}, u32[]{:S(2)}) async-start(s32[128,1,1]{2,1,0:T(1,128)} %copy.36), calls=%async_computation.1 | async-start | bytes 131072 | tf_op jit(solution)/shard_map/all_to_all | solution.py:119
  91.1 526.6 %all-to-all-start.2 = ((bf16[128,128,1024]{2,1,0:T(8,128)(2,1)}), bf16[128,128,1024]{2,1,0:T(8,128)(2,1)}, u32[]{:S(2)}, u32[]{:S(2)}) async-start(bf16[128,128,1024]{2,1,0:T(8,128)(2,1)} %copy.38), calls=%async_computation.2 | async-start | bytes 67108864 | tf_op jit(solution)/shard_map/all_to_all | solution.py:118
  658.2 52.8 %all-to-all-start.3 = ((f32[128,1,128]{2,1,0:T(1,128)}), f32[128,1,128]{2,1,0:T(1,128)S(1)}, u32[]{:S(2)}, u32[]{:S(2)}) async-start(f32[128,1,128]{2,1,0:T(1,128)} %bitcast.13), calls=%async_computation.3 | async-start | bytes 131072 | tf_op jit(solution)/shard_map/all_to_all | solution.py:125
where the time goes:
time: 713 us; the launch traced here: 712 us
  waiting for transfers between devices  464 us (65%)
  matrix products  94.7 us (13%)
  starting transfers between devices  74.9 us (11%)
  local copies, waits for them, and re-layouts  59.3 us (8%)
  other arithmetic  16.3 us (2%)
    all_to_all x1, waiting for transfers between devices, on_device(): lax.all_to_all(outgoing, 'shard', split_axis=0, concat_axis=0, tiled=True)  455 us
    all_to_all x1, starting transfers between devices, on_device(): lax.all_to_all(row_max, 'shard', split_axis=0, concat_axis=0, tiled=True)  43.4 us
    dot_general x1, matrix products, pair_maxima(): jnp.einsum('pid,pjd->pij', rows, cols, preferred_element_type=jnp.float32)  40.5 us
    dot_general x2, matrix products, select_tiles(): jnp.dot(selector.astype(jnp.bfloat16), unit.reshape(blocks, width * depth...  31.8 us
    dot_general x1, local copies, waits for them, and re-layouts, select_tiles(): jnp.dot(selector.astype(jnp.bfloat16), unit.reshape(blocks, width * depth...  30.7 us
    dot_general x4, matrix products, tile(): lax.dot_general(query, flat, (((1,), (1,)), ((), ())), preferred_element_...  21.9 us
  transfers between devices with their start and end apart: 4, of which 2 were waited for; matrix products, arithmetic and copies ran while one was open for 17% of the time, Pallas kernels for 0%

commit v1 on v0

v1 whole, which is shorter than its diff:
```python
import functools

import jax
import jax.numpy as jnp
from jax import lax
from jax.experimental import pallas as pl
from jax.experimental.pallas import tpu as pltpu
from jax.sharding import PartitionSpec as P

PARTS = 2


def normalize_kernel(values_ref, unit_ref):
    values = values_ref[...].astype(jnp.float32)
    total = jnp.sum(values * values, axis=-1, keepdims=True)
    unit_ref[...] = (values * lax.rsqrt(total + 1e-06)).astype(jnp.bfloat16)


def normalize(embeddings):
    rows, depth = embeddings.shape
    step = 256
    return pl.pallas_call(
        normalize_kernel,
        grid=(rows // step,),
        in_specs=[pl.BlockSpec((step, depth), lambda i: (i, 0))],
        out_specs=pl.BlockSpec((step, depth), lambda i: (i, 0)),
        out_shape=jax.ShapeDtypeStruct((rows, depth), jnp.bfloat16),
        name="normalize",
    )(embeddings)


def pack_kernel(group, chosen, unit_ref, out_ref):
    base = pl.program_id(0) * group
    for k in range(group):
        out_ref[k] = unit_ref[chosen[base + k]]


def pack(chosen, unit, part):
    blocks, width, depth = unit.shape
    slots = chosen.shape[0]
    rows = width // PARTS
    group = 8
    return pl.pallas_call(
        functools.partial(pack_kernel, group),
        grid_spec=pltpu.PrefetchScalarGridSpec(
            num_scalar_prefetch=1,
            grid=(slots // group,),
            in_specs=[pl.BlockSpec((blocks, rows, depth), lambda i, c: (0, part, 0))],
            out_specs=pl.BlockSpec((group, rows, depth), lambda i, c: (i, 0, 0)),
        ),
        out_shape=jax.ShapeDtypeStruct((slots, rows, depth), jnp.bfloat16),
        compiler_params=pltpu.CompilerParams(vmem_limit_bytes=40 * 1024 * 1024),
        name="pack",
    )(chosen, unit)


def score_kernel(group, first, mine, mine_rows, theirs_rows, unit_ref, arrived_ref, back_ref, best_ref, held):
    step = pl.program_id(0)
    blocks, width, _ = unit_ref.shape
    rows = arrived_ref.shape[1]

    @pl.when(step == 0)
    def _():
        held[...] = jnp.full(held.shape, -1.0, jnp.float32)

    i = lax.broadcasted_iota(jnp.int32, (width, rows), 0)
    j = lax.broadcasted_iota(jnp.int32, (width, rows), 1) + first
    back_ref[...] = jnp.full(back_ref.shape, -1.0, jnp.float32)
    for k in range(group):
        slot = step * group + k

        @pl.when(theirs_rows[slot] > first)
        def _():
            block = mine[slot]
            scores = lax.dot_general(
                unit_ref[block], arrived_ref[k], (((1,), (1,)), ((), ())), preferred_element_type=jnp.float32
            )
            keep = (i < mine_rows[slot]) & (j < theirs_rows[slot])
            scores = jnp.where(keep, scores, -1.0)
            back_ref[pl.ds(k, 1), :] = jnp.max(scores, axis=0, keepdims=True)
            held[block] = jnp.maximum(held[block], scores)

    @pl.when(step == pl.num_programs(0) - 1)
    def _():
        for b in range(blocks):
            best_ref[pl.ds(b, 1), :] = jnp.max(held[b].T, axis=0, keepdims=True)


def score(first, mine, mine_rows, theirs_rows, unit, arrived):
    blocks, width, depth = unit.shape
    slots, rows, _ = arrived.shape
    group = 8
    return pl.pallas_call(
        functools.partial(score_kernel, group, first),
        grid_spec=pltpu.PrefetchScalarGridSpec(
            num_scalar_prefetch=3,
            grid=(slots // group,),
            in_specs=[
                pl.BlockSpec((blocks, width, depth), lambda i, *_: (0, 0, 0)),
                pl.BlockSpec((group, rows, depth), lambda i, *_: (i, 0, 0)),
            ],
            out_specs=[
                pl.BlockSpec((group, rows), lambda i, *_: (i, 0)),
                pl.BlockSpec((blocks, width), lambda i, *_: (0, 0)),
            ],
            scratch_shapes=[pltpu.VMEM((blocks, width, rows), jnp.float32)],
        ),
        out_shape=[
            jax.ShapeDtypeStruct((slots, rows), jnp.float32),
            jax.ShapeDtypeStruct((blocks, width), jnp.float32),
        ],
        compiler_params=pltpu.CompilerParams(vmem_limit_bytes=40 * 1024 * 1024),
        name="score",
    )(mine, mine_rows, theirs_rows, unit, arrived)


def one_hot(index, count, valid):
    return (index[:, None] == jnp.arange(count, dtype=jnp.int32)[None, :]) & valid[:, None]


def pick(index, values):
    hit = index[:, None] == jnp.arange(values.shape[-1], dtype=jnp.int32)[None, :]
    return jnp.sum(jnp.where(hit, values, 0), axis=1)


def fold_maxima(selector, maxima):
    spread = jnp.where(selector[:, :, None], maxima[:, None, :], -1.0)
    return spread.max(axis=0)


def local_maxima(unit, block_rows, linked):
    blocks, width, depth = unit.shape
    total = blocks * width
    flat = unit.reshape(total, depth)
    live_flat = (jnp.arange(width, dtype=jnp.int32)[None, :] < block_rows[:, None]).reshape(total)
    linked_rows = jnp.repeat(linked, width, axis=0)
    span = min(512, total)
    columns = jnp.arange(total, dtype=jnp.int32)

    def tile(number):
        start = number * span
        query = lax.dynamic_slice_in_dim(flat, start, span, 0)
        scores = lax.dot_general(query, flat, (((1,), (1,)), ((), ())), preferred_element_type=jnp.float32)
        ids = start + jnp.arange(span, dtype=jnp.int32)
        link = jnp.repeat(lax.dynamic_slice_in_dim(linked_rows, start, span, 0), width, axis=1)
        keep = link & live_flat[None, :] & lax.dynamic_slice_in_dim(live_flat, start, span, 0)[:, None]
        keep = keep & (ids[:, None] != columns[None, :])
        return jnp.where(keep, scores, -1.0).max(axis=1)

    result = lax.map(tile, jnp.arange(total // span, dtype=jnp.int32))
    return result.reshape(blocks, width)


def on_device(embeddings, block_rows, pairs):
    blocks = block_rows.shape[0]
    width = embeddings.shape[0] // blocks
    peers = lax.axis_size("shard")
    myself = lax.axis_index("shard")
    row_block, col_block = pairs[:, 0], pairs[:, 1]
    alive = pairs[:, 2] == myself
    owner = row_block // blocks
    remote = alive & (owner != myself)
    row_local, col_local = row_block % blocks, col_block % blocks
    code = row_local * blocks + col_local
    wanted = jnp.max(jnp.where(one_hot(owner, peers, remote), code[:, None], -1), axis=0)
    told = lax.all_gather(jnp.concatenate([wanted, block_rows])[None], "shard", axis=0, tiled=True)

    unit = normalize(embeddings).reshape(blocks, width, -1)
    chosen = jnp.maximum(wanted, 0) % blocks
    arrived = []
    for part in range(PARTS):
        outgoing = pack(chosen, unit, part)
        arrived.append(lax.all_to_all(outgoing, "shard", split_axis=0, concat_axis=0, tiled=True))

    asked = lax.dynamic_slice_in_dim(told, myself, 1, 1)[:, 0]
    valid = asked >= 0
    mine = jnp.maximum(asked, 0) // blocks
    theirs_rows = jnp.where(valid, pick(jnp.maximum(asked, 0) % blocks, told[:, peers:]), 0)
    mine_rows = pick(mine, block_rows[None, :])

    nearby = alive & ~remote
    row_table = one_hot(row_local, blocks, nearby).astype(jnp.float32)
    col_table = one_hot(col_local, blocks, nearby).astype(jnp.float32)
    adjacency = (
        lax.dot_general(row_table, col_table, (((0,), (0,)), ((), ())), preferred_element_type=jnp.float32) > 0.5
    )
    best = local_maxima(unit, block_rows, adjacency | adjacency.T)

    back = []
    for part in range(PARTS):
        part_back, part_best = score(
            part * (width // PARTS), mine, mine_rows, theirs_rows, unit, arrived[part]
        )
        back.append(part_back)
        best = jnp.maximum(best, part_best)
    returned = lax.all_to_all(
        jnp.concatenate(back, axis=1), "shard", split_axis=0, concat_axis=0, tiled=True
    )
    return jnp.maximum(best, fold_maxima(one_hot(chosen, blocks, wanted >= 0), returned))


def solution(mesh):
    placed = (P("shard", None), P("shard"), P("shard", None))
    return jax.shard_map(
        on_device, mesh=mesh, in_specs=placed, out_specs=P("shard", None), check_vma=False
    )
```

time: 713 us -> 664 us (0.931)
  matrix products: 94.7 us -> 22.5 us
  Pallas kernels: 0 us -> 72.1 us
  local copies, waits for them, and re-layouts: 59.3 us -> 18.9 us
  starting transfers between devices: 74.9 us -> 40.4 us
  waiting for transfers between devices: 464 us -> 487 us
  between operations: 0.17 us -> 13.6 us
  other arithmetic: 16.3 us -> 5.52 us
    unnamed x0 -> x2, waiting for transfers between devices: none -> 262 us
    all_to_all x1 -> x2, waiting for transfers between devices: 455 us -> 216 us  [on_device(): lax.all_to_all(outgoing, 'shard', split_axis=0, concat_axis=0, tiled=True)]
    dot_general x3 -> x0, matrix products: 72.2 us -> none  [the longest x1 40.5 us: pair_maxima(): jnp.einsum('pid,pjd->pij', rows, cols, preferred_element_type=jnp.float32)]
    pallas_call x0 -> x5, Pallas kernels: none -> 72.1 us  [the longest x2 42.9 us: score(): pl.pallas_call(functools.partial(score_kernel, group, first), grid_spec=p...]
    all_to_all x3 -> x1, starting transfers between devices: 64.7 us -> 6.51 us  [on_device(): lax.all_to_all(jnp.concatenate(back, axis=1), 'shard', split_axis=0, conc...]
    dot_general x1 -> x0, local copies, waits for them, and re-layouts: 30.7 us -> none  [select_tiles(): jnp.dot(selector.astype(jnp.bfloat16), unit.reshape(blocks, width * depth...]
    all_to_all x1 -> x2, starting transfers between devices: 10.2 us -> 33.9 us  [on_device(): lax.all_to_all(outgoing, 'shard', split_axis=0, concat_axis=0, tiled=True)]
  transfers between devices with their start and end apart: 4 -> 4, of which waited for: 2 -> 3; matrix products, arithmetic and copies ran while one was open for 17% -> 6% of each run, Pallas kernels for 0% -> 5%
where the time goes in v1:
time: 664 us; the launch traced here: 663 us
  waiting for transfers between devices  487 us (73%)
  Pallas kernels  72.1 us (11%)
  starting transfers between devices  40.4 us (6%)
  matrix products  22.5 us (3%)
  local copies, waits for them, and re-layouts  18.9 us (3%)
  between operations  13.6 us (2%)
    unnamed x2, waiting for transfers between devices  262 us
    all_to_all x2, waiting for transfers between devices, on_device(): lax.all_to_all(outgoing, 'shard', split_axis=0, concat_axis=0, tiled=True)  216 us
    pallas_call x2, Pallas kernels, score(): pl.pallas_call(functools.partial(score_kernel, group, first), grid_spec=p...  42.9 us
    all_to_all x2, starting transfers between devices, on_device(): lax.all_to_all(outgoing, 'shard', split_axis=0, concat_axis=0, tiled=True)  33.9 us
    pallas_call x2, Pallas kernels, pack(): pl.pallas_call(functools.partial(pack_kernel, group), grid_spec=pltpu.Pre...  22 us
    dot_general x4, matrix products, tile(): lax.dot_general(query, flat, (((1,), (1,)), ((), ())), preferred_element_...  21.9 us
    broadcast_in_dim x4, local copies, waits for them, and re-layouts, tile(): jnp.repeat(lax.dynamic_slice_in_dim(linked_rows, start, span, 0), width,...  13.9 us
  transfers between devices with their start and end apart: 4, of which 3 were waited for; matrix products, arithmetic and copies ran while one was open for 6% of the time, Pallas kernels for 5%

profile of v1, /device:TPU:1, one launch (start us, length us, event | category | flops | bytes accessed | tf_op | source)
XLA Modules:
  0.0 662.8 jit_solution(5893598985839995118)
XLA Ops:
  6.5 0.8 compare_and_fusion
  7.3 0.7 and_reduce_fusion
  8.1 0.7 multiply_add_fusion
  9.1 7.2 %normalize.1 = bf16[2048,1024]{1,0:T(8,128)(2,1)} custom-call(bf16[2048,1024]{1,0:T(8,128)(2,1)} %values_ref.1), custom_call_target="tpu_custom_call" | custom-call | tf_op jit(solution)/shard_map/normalize/pallas_call | solution.py:22
  16.3 11.1 %pack.2 = bf16[128,64,1024]{2,1,0:T(8,128)(2,1)} custom-call(s32[128]{0:T(128)S(1)} %and_select_fusion.3.chosen, bf16[16,128,1024]{2,1,0:T(8,128)(2,1)} %bitcast.38), custom_call_target="tpu_custom_call" | custom-call | tf_op jit(solution)/shard_map/pack/pallas_call | solution.py:43
  27.3 12.0 %all-to-all-start = ((bf16[128,64,1024]{2,1,0:T(8,128)(2,1)}), bf16[128,64,1024]{2,1,0:T(8,128)(2,1)}, u32[]{:S(2)}, u32[]{:S(2)}) async-start(bf16[128,64,1024]{2,1,0:T(8,128)(2,1)} %pack.2), calls=%async_computation | async-start | bytes 33554432 | tf_op jit(solution)/shard_map/all_to_all | solution.py:173
  39.3 11.0 %pack.3 = bf16[128,64,1024]{2,1,0:T(8,128)(2,1)} custom-call(s32[128]{0:T(128)S(1)} %and_select_fusion.3.chosen, bf16[16,128,1024]{2,1,0:T(8,128)(2,1)} %bitcast.39), custom_call_target="tpu_custom_call" | custom-call | tf_op jit(solution)/shard_map/pack/pallas_call | solution.py:43
  50.3 215.9 %all-to-all-done.arrived_ref = bf16[128,64,1024]{2,1,0:T(8,128)(2,1)} async-done(((bf16[128,64,1024]{2,1,0:T(8,128)(2,1)}), bf16[128,64,1024]{2,1,0:T(8,128)(2,1)}, u32[]{:S(2)}, u32[]{:S(2)}) %all-to-all-start) | async-done | bytes 16777248 | tf_op jit(solution)/shard_map/all_to_all | solution.py:173
  266.2 21.9 %all-to-all-start.1 = ((bf16[128,64,1024]{2,1,0:T(8,128)(2,1)}), bf16[128,64,1024]{2,1,0:T(8,128)(2,1)}, u32[]{:S(2)}, u32[]{:S(2)}) async-start(bf16[128,64,1024]{2,1,0:T(8,128)(2,1)} %pack.3), calls=%async_computation.1 | async-start | bytes 33554432 | tf_op jit(solution)/shard_map/all_to_all | solution.py:173
  288.3 0.6 copy-done
  289.0 0.5 convolution_compare_fusion
  289.8 42.2 %while.11 = (s32[]{:T(128)}, f32[4,512]{1,0:T(4,128)S(1)}, s32[4]{0:T(128)S(1)}, pred[2048,16]{1,0:T(8,128)(4,1)S(1)}, pred[2048]{0:T(1024)(128)(4,1)S(1)}, /*in...) while((s32[]{:T(128)}, f32[4,512]{1,0:T(4,128)S(1)}, ...), condition=%wide.region_2.3_spmd.clone, body=%wide.region_0.2_spmd.clone.sunk | while | flops 2153777152 | bytes 7380731 | solution.py:150
  289.8 0.7 dynamic_slice.41
  291.2 3.5 broadcast_in_dim.124
  294.8 5.5 select_reduce_fusion.5
  300.4 0.7 dynamic_slice.41
  301.7 3.5 broadcast_in_dim.124
  305.4 5.5 select_reduce_fusion.5
  310.9 0.7 dynamic_slice.41
  312.3 3.5 broadcast_in_dim.124
  315.9 5.5 select_reduce_fusion.5
  321.5 0.7 dynamic_slice.41
  322.8 3.5 broadcast_in_dim.124
  326.5 5.5 select_reduce_fusion.5
  332.0 261.7 %all-reduce.3.cloned.1.call-done = s32[18432]{0:T(1024)} async-done(((s32[18432]{0:T(1024)}), s32[18432]{0:T(1024)}) %all-reduce.3.cloned.1.call-update) | async-done | bytes 73744
  593.8 1.0 reshape.95
  595.5 21.5 %score.2 = (f32[128,64]{1,0:T(8,128)S(1)}, f32[16,128]{1,0:T(8,128)S(1)}) custom-call(s32[128]{0:T(128)S(1)} %add_select_fusion.2.mine, s32[128]{0:T(128)S(1)} %get-tuple-element.101.mine_rows, s32[128]{0:T(128)S(1)} %broadcast_select_fusion.theirs_rows, bf16[16,128,1024]{2,1,0:T(8,128)(2,1)} %bitcast.40, bf16[128,64,1024]{2,1,0:T(8,128)(2,1)} %all-to-all-done.arrived_ref), custom_call_target="tpu_custom_call" | custom-call | tf_op jit(solution)/shard_map/score/pallas_call | solution.py:93
  617.1 21.3 %score.3 = (f32[128,64]{1,0:T(8,128)S(1)}, f32[16,128]{1,0:T(8,128)S(1)}) custom-call(s32[128]{0:T(128)S(1)} %add_select_fusion.2.mine, s32[128]{0:T(128)S(1)} %get-tuple-element.101.mine_rows, s32[128]{0:T(128)S(1)} %broadcast_select_fusion.theirs_rows, bf16[16,128,1024]{2,1,0:T(8,128)(2,1)} %bitcast.41, bf16[128,64,1024]{2,1,0:T(8,128)(2,1)} %all-to-all-done.1.arrived_ref), custom_call_target="tpu_custom_call" | custom-call | tf_op jit(solution)/shard_map/score/pallas_call | solution.py:93
  638.4 0.7 pad_maximum_fusion
  639.1 6.5 all-to-all-start.2
  645.7 9.2 %all-to-all-done.2 = f32[128,1,128]{2,1,0:T(1,128)S(1)} async-done(((f32[128,1,128]{2,1,0:T(1,128)}), f32[128,1,128]{2,1,0:T(1,128)S(1)}, u32[]{:S(2)}, u32[]{:S(2)}) %all-to-all-start.2) | async-done | bytes 65568 | tf_op jit(solution)/shard_map/all_to_all | solution.py:196
  655.3 0.6 maximum_maximum_fusion
  (46 shorter events, 2.8 us)
Async XLA Ops:
  27.3 238.8 %all-to-all-start = ((bf16[128,64,1024]{2,1,0:T(8,128)(2,1)}), bf16[128,64,1024]{2,1,0:T(8,128)(2,1)}, u32[]{:S(2)}, u32[]{:S(2)}) async-start(bf16[128,64,1024]{2,1,0:T(8,128)(2,1)} %pack.2), calls=%async_computation | async-start | bytes 33554432 | tf_op jit(solution)/shard_map/all_to_all | solution.py:173
  50.3 237.9 %copy-start.1 = (s32[16]{0:T(128)S(1)}, s32[16]{0:T(128)}, u32[]{:S(2)}) copy-start(s32[16]{0:T(128)} %param.6) | copy-start | bytes 196
  266.2 350.9 %all-to-all-start.1 = ((bf16[128,64,1024]{2,1,0:T(8,128)(2,1)}), bf16[128,64,1024]{2,1,0:T(8,128)(2,1)}, u32[]{:S(2)}, u32[]{:S(2)}) async-start(bf16[128,64,1024]{2,1,0:T(8,128)(2,1)} %pack.3), calls=%async_computation.1 | async-start | bytes 33554432 | tf_op jit(solution)/shard_map/all_to_all | solution.py:173
  288.1 305.6 %all-reduce.3.cloned.1.call-start = ((), (), s32[]{:S(2)}) async-start(), calls=%async_computation.3 | async-start | bytes 147456
  288.3 0.6 copy-start
  639.1 15.9 %all-to-all-start.2 = ((f32[128,1,128]{2,1,0:T(1,128)}), f32[128,1,128]{2,1,0:T(1,128)S(1)}, u32[]{:S(2)}, u32[]{:S(2)}) async-start(f32[128,1,128]{2,1,0:T(1,128)} %bitcast.9), calls=%async_computation.2 | async-start | bytes 131072 | tf_op jit(solution)/shard_map/all_to_all | solution.py:196
Sparse Core Ops, SparseCore 0:
  293.7 300.0 all-reduce.2

commit v2 on v1

v2 whole, which is shorter than its diff:
```python
import functools

import jax
import jax.numpy as jnp
import numpy as np
from jax import lax
from jax.experimental import pallas as pl
from jax.experimental.pallas import tpu as pltpu
from jax.sharding import PartitionSpec as P

UNIT = 16
ITEM = 4
SHARE = 8
MIB = 1024 * 1024


def normalize_kernel(values_ref, unit_ref):
    values = values_ref[...].astype(jnp.float32)
    total = jnp.sum(values * values, axis=-1, keepdims=True)
    unit_ref[...] = (values * lax.rsqrt(total + 1e-06)).astype(jnp.bfloat16)


def normalize(embeddings):
    rows, depth = embeddings.shape
    step = 256
    return pl.pallas_call(
        normalize_kernel,
        grid=(rows // step,),
        in_specs=[pl.BlockSpec((step, depth), lambda i: (i, 0))],
        out_specs=pl.BlockSpec((step, depth), lambda i: (i, 0)),
        out_shape=jax.ShapeDtypeStruct((rows, depth), jnp.bfloat16),
        name="normalize",
    )(embeddings)


def nearby_kernel(first, second, linked, counts, unit_ref, best_ref, held):
    step = pl.program_id(0)
    blocks = best_ref.shape[0]
    width = 128

    @pl.when(step == 0)
    def _():
        held[...] = jnp.full(held.shape, -1.0, jnp.float32)
        best_ref[...] = jnp.full(best_ref.shape, -1.0, jnp.float32)

    left, right = first[step], second[step]
    i = lax.broadcasted_iota(jnp.int32, (width, width), 0)
    j = lax.broadcasted_iota(jnp.int32, (width, width), 1)
    rows = unit_ref[pl.ds(pl.multiple_of(left * 256, 256), 256), :]
    cols = unit_ref[pl.ds(pl.multiple_of(right * 256, 256), 256), :]
    scores = lax.dot_general(rows, cols, (((1,), (1,)), ((), ())), preferred_element_type=jnp.float32)
    for a in range(2):
        for b in range(2):
            r, c = left * 2 + a, right * 2 + b
            limit = jnp.where(linked[r * blocks + c] > 0, counts[r], 0)
            keep = (i < limit) & (j < counts[c]) & ((r != c) | (i != j))
            part = jnp.where(keep, scores[a * width : (a + 1) * width, b * width : (b + 1) * width], -1.0)
            held[r] = jnp.maximum(held[r], part)
            best_ref[pl.ds(c, 1), :] = jnp.maximum(best_ref[pl.ds(c, 1), :], jnp.max(part, axis=0, keepdims=True))

    @pl.when(step == pl.num_programs(0) - 1)
    def _():
        for b in range(blocks):
            best_ref[pl.ds(b, 1), :] = jnp.maximum(
                best_ref[pl.ds(b, 1), :], jnp.max(held[b].T, axis=0, keepdims=True)
            )


def nearby_maxima(unit, counts, linked):
    rows, depth = unit.shape
    blocks = counts.shape[0]
    sides = rows // 256
    first, second = np.triu_indices(sides)
    return pl.pallas_call(
        nearby_kernel,
        grid_spec=pltpu.PrefetchScalarGridSpec(
            num_scalar_prefetch=4,
            grid=(len(first),),
            in_specs=[pl.BlockSpec((rows, depth), lambda i, *_: (0, 0))],
            out_specs=pl.BlockSpec((blocks, rows // blocks), lambda i, *_: (0, 0)),
            scratch_shapes=[pltpu.VMEM((blocks, 128, 128), jnp.float32)],
        ),
        out_shape=jax.ShapeDtypeStruct((blocks, rows // blocks), jnp.float32),
        compiler_params=pltpu.CompilerParams(vmem_limit_bytes=32 * MIB),
        name="nearby",
    )(
        jnp.asarray(first, jnp.int32),
        jnp.asarray(second, jnp.int32),
        linked.astype(jnp.int32).reshape(-1),
        counts,
        unit,
    )


def exact_dot(a, b):
    return jnp.dot(
        a.astype(jnp.float32).astype(jnp.bfloat16),
        b.astype(jnp.float32).astype(jnp.bfloat16),
        preferred_element_type=jnp.float32,
    ).astype(jnp.int32)


def flip(a):
    return a.astype(jnp.float32).T.astype(jnp.int32)


def plan_kernel(
    direct, items, chips, me_ref, pair_ref, count_ref, count_t_ref,
    send_ref, far_ref, seg_ref, far_seg_ref, hand_ref, target_ref, back_ref, fits_ref,
    w_lo, w_hi, sums, mine,
):
    device = me_ref[0]
    chip, core = device // 2, device % 2
    devices = 2 * chips
    flat = (chips, chips)
    pair = pair_ref[...]
    code = jnp.maximum(pair, 0)
    row_of, col_of = code >> 4, code & 15
    row_count = jnp.zeros(pair.shape, jnp.int32)
    col_count = jnp.zeros(pair.shape, jnp.int32)
    for l in range(16):
        row_count = jnp.where(row_of == l, count_t_ref[pl.ds(l, 1), :], row_count)
        col_count = jnp.where(col_of == l, count_ref[:, l : l + 1], col_count)

    xs = lax.broadcasted_iota(jnp.int32, (chips, devices), 0)
    ds = lax.broadcasted_iota(jnp.int32, (chips, devices), 1)
    pick = [(ds == 2 * xs + i).astype(jnp.int32) for i in range(2)]
    pick_t = [flip(p) for p in pick]

    def split(values):
        half = [exact_dot(p, values) for p in pick]
        return [[exact_dot(half[i], pick_t[j]) for j in range(2)] for i in range(2)]

    asked = {"code": split(pair + 1), "row": split(row_count), "col": split(col_count)}
    asked_t = {k: [[flip(v[j][i]) for j in range(2)] for i in range(2)] for k, v in asked.items()}

    x = lax.broadcasted_iota(jnp.int32, flat, 0)
    y = lax.broadcasted_iota(jnp.int32, flat, 1)
    low, same = x <= y, x == y
    edges = []
    for kind in range(2):
        for p in range(2):
            for q in range(2):
                first, second = (asked_t, asked) if kind == 0 else (asked, asked_t)
                here = {k: jnp.where(low, first[k][p][q], second[k][q][p]) for k in asked}
                exists = here["code"] > 0
                if kind == 1:
                    exists = exists & ~same
                number = jnp.maximum(here["code"] - 1, 0)
                r, c = number >> 4, number & 15
                side = jnp.where(low, p, q) * 16
                other = jnp.where(low, q, p) * 16
                owns_row = low if kind == 0 else ~low
                own_block = side + jnp.where(owns_row, r, c)
                other_block = other + jnp.where(owns_row, c, r)
                own_rows = jnp.where(exists, jnp.where(owns_row, here["row"], here["col"]), 0)
                other_rows = jnp.where(exists, jnp.where(owns_row, here["col"], here["row"]), 0)
                edges.append((exists, own_block, other_block, own_rows, other_rows))
    for e, (exists, _, _, own_rows, other_rows) in enumerate(edges):
        own_units, other_units = (own_rows + 15) >> 4, (other_rows + 15) >> 4
        w_lo[e] = jnp.where(low, own_units, other_units)
        w_hi[e] = jnp.where(low, other_units, own_units)

    for half in range(2):
        for choice in range(16):
            up = jnp.zeros(flat, jnp.int32)
            down = jnp.zeros(flat, jnp.int32)
            for b in range(4):
                if choice >> b & 1:
                    up = up + w_lo[half * 4 + b]
                else:
                    down = down + w_hi[half * 4 + b]
            sums[half, choice] = up
            sums[2 + half, choice] = down

    def try_half(a, least):
        up_a, down_a = sums[0, a], sums[2, a]
        for b in range(16):
            up, down = up_a + sums[1, b], down_a + sums[3, b]
            over_up, over_down = jnp.maximum(up - 2 * direct, 0), jnp.maximum(down - 2 * direct, 0)
            far = ((over_up + 3) >> 2) + ((over_down + 3) >> 2)
            rank = (((far * 64 + over_up + over_down) * 128) + jnp.maximum(up, down)) * 256 + (b * 16 + a)
            least = jnp.minimum(least, rank)
        return least

    least = lax.fori_loop(0, 16, try_half, jnp.full(flat, 2**30, jnp.int32))
    chosen = jnp.where(same, 255, least & 255)

    out_total = jnp.zeros(flat, jnp.int32)
    in_total = jnp.zeros(flat, jnp.int32)
    for e, (exists, own_block, other_block, own_rows, other_rows) in enumerate(edges):
        bit = (chosen >> e) & 1
        sends = exists & ((bit == 1) == low)
        out_units = jnp.where(sends, (own_rows + 15) >> 4, 0)
        in_rows = jnp.where(same, own_rows, other_rows)
        in_units = jnp.where((exists & ~sends) | same, (in_rows + 15) >> 4, 0)
        out_total = out_total + out_units
        in_total = in_total + in_units
        mine[e] = out_units
        mine[8 + e] = own_block ^ (core * 16)
        mine[16 + e] = in_units
        mine[24 + e] = jnp.where(same, other_block, own_block) ^ (core * 16)
        mine[32 + e] = in_rows
    mine[40] = out_total
    mine[41] = in_total

    over = jnp.maximum(out_total - 2 * direct, 0)
    far = (over + 3) >> 2
    before = exact_dot(far, (x < y).astype(jnp.int32))
    total = jnp.sum(far, axis=1, keepdims=True)
    at_self = jnp.sum(jnp.where(same, before, 0), axis=1, keepdims=True)
    rank = before - at_self + jnp.where(y < x, total, 0)
    number, place = [], []
    worst = jnp.max((total + 1) >> 1)
    for k in range(2):
        number.append((far + ((rank & 1) == k).astype(jnp.int32)) >> 1)
        place.append(exact_dot((y < x).astype(jnp.int32), number[k]))
        worst = jnp.maximum(worst, jnp.max(jnp.sum(number[k], axis=0, keepdims=True)))
    fits_ref[0] = (worst <= items).astype(jnp.int32)
    odd = core == 1
    number = jnp.where(odd, number[1], number[0])
    place = jnp.where(odd, place[1], place[0])
    skip = ((rank & 1) != core).astype(jnp.int32)
    number_t, place_t, rank_t, skip_t, far_t = flip(number), flip(place), flip(rank), flip(skip), flip(far)
    for k, v in enumerate((number, rank, skip, far, number_t, place_t, rank_t, skip_t, far_t)):
        mine[42 + k] = v
    own = pl.ds(chip, 1)

    out_units = [mine[e, own, :] for e in range(SHARE)]
    out_block = [mine[8 + e, own, :] for e in range(SHARE)]
    in_units = [mine[16 + e, own, :] for e in range(SHARE)]
    in_block = [mine[24 + e, own, :] for e in range(SHARE)]
    in_rows = [mine[32 + e, own, :] for e in range(SHARE)]
    out_total, in_total = mine[40, own, :], mine[41, own, :]
    number, rank, skip, far, number_t, place_t, rank_t, skip_t, far_t = (mine[42 + k, own, :] for k in range(9))

    def lane(total):
        plain = jnp.minimum(total, 2 * direct)
        half = (plain + 1) >> 1
        return jnp.where(odd, half, 0), jnp.where(odd, plain - half, half)

    def unit_at(position, valid):
        value = jnp.full(position.shape, -1, jnp.int32)
        start = jnp.zeros((1, chips), jnp.int32)
        for e in range(SHARE):
            hit = valid & (position >= start) & (position < start + out_units[e])
            value = jnp.where(hit, out_block[e] * 8 + position - start, value)
            start = start + out_units[e]
        return value

    begin, length = lane(out_total)
    step = lax.broadcasted_iota(jnp.int32, (direct, chips), 0)
    plain = unit_at(begin + step, step < length)
    send_ref[...] = jnp.maximum(plain, 0)
    target_ref[pl.ds(0, direct), :] = plain

    begin, length = lane(in_total)
    start = jnp.zeros((1, chips), jnp.int32)
    starts = []
    for e in range(SHARE):
        starts.append(start)
        top = jnp.maximum(start, begin) - begin
        end = jnp.minimum(start + in_units[e], begin + length) - begin
        last = jnp.minimum(UNIT * end, UNIT * (start - begin) + in_rows[e])
        seg_ref[pl.ds(e, 1), :] = jnp.where(end > top, (in_block[e] << 16) + (top << 10) + last, 0)
        start = start + in_units[e]

    if items:
        slot = lax.broadcasted_iota(jnp.int32, (items, chips), 0)
        sixteen = lax.broadcasted_iota(jnp.int32, (16, chips), 0) + 2 * direct
        beyond = unit_at(sixteen, sixteen < out_total)
        for p in range(ITEM):
            value = jnp.zeros((items, 1), jnp.int32)
            for t in range(4):
                hit = (rank + t == 2 * slot + core) & (t < far)
                row = jnp.maximum(beyond[4 * t + p : 4 * t + p + 1], 0)
                value = value + jnp.sum(jnp.where(hit, row, 0), axis=1, keepdims=True)
            far_ref[:, p : p + 1] = value
        for k in range(2):
            for p in range(ITEM):
                even, uneven = beyond[8 * k + p : 8 * k + p + 1], beyond[8 * k + 4 + p : 8 * k + 5 + p]
                target_ref[pl.ds(direct + 4 * k + p, 1), :] = jnp.where(
                    k < number, jnp.where(skip == 0, even, uneven), -1
                )
            back_ref[pl.ds(k, 1), :] = jnp.where(k < number_t, place_t + k, -1)
        hits = [
            (place_t + (t >> 1) == slot) & ((t & 1) == skip_t) & (t < far_t) for t in range(4)
        ]
        for e in range(SHARE):
            value = jnp.zeros((items, 1), jnp.int32)
            for t in range(4):
                offset = starts[e] - (2 * direct + 4 * t)
                top = jnp.clip(offset, 0, 4)
                end = jnp.clip(offset + in_units[e], 0, 4)
                last = jnp.minimum(UNIT * end, UNIT * offset + in_rows[e])
                made = jnp.where(end > top, (in_block[e] << 16) + (top << 10) + last, 0)
                value = value + jnp.sum(jnp.where(hits[t], made, 0), axis=1, keepdims=True)
            far_seg_ref[:, e : e + 1] = value
        number_t, place_t, rank_t, skip_t = (mine[42 + k] for k in (4, 5, 6, 7))
        for q in range(items):
            value = jnp.zeros(flat, jnp.int32)
            for k in range(2):
                hit = (place_t + k == q) & (k < number_t)
                value = value + jnp.where(hit, y * items + ((rank_t + skip_t + 2 * k) >> 1), 0)
            hand_ref[:, q : q + 1] = jnp.sum(value, axis=1, keepdims=True)


def make_plan(direct, items, told, device):
    devices, columns = told.shape
    chips = devices // 2
    blocks = columns - devices
    ints = lambda *shape: jax.ShapeDtypeStruct(shape, jnp.int32)
    vmem = pl.BlockSpec(memory_space=pltpu.VMEM)
    some = max(items, 8)
    return pl.pallas_call(
        functools.partial(plan_kernel, direct, items, chips),
        in_specs=[pl.BlockSpec(memory_space=pltpu.SMEM), vmem, vmem, vmem],
        out_specs=[vmem] * 7 + [pl.BlockSpec(memory_space=pltpu.SMEM)],
        out_shape=[
            ints(direct, chips),
            ints(some, ITEM),
            ints(SHARE, chips),
            ints(some, SHARE),
            ints(chips, some),
            ints(direct + 8, chips),
            ints(2, chips),
            ints(1),
        ],
        scratch_shapes=[
            pltpu.VMEM((SHARE, chips, chips), jnp.int32),
            pltpu.VMEM((SHARE, chips, chips), jnp.int32),
            pltpu.VMEM((4, 16, chips, chips), jnp.int32),
            pltpu.VMEM((51, chips, chips), jnp.int32),
        ],
        compiler_params=pltpu.CompilerParams(vmem_limit_bytes=32 * MIB),
        name="plan",
    )(device.reshape(1), told[:, :devices], told[:, devices:], told[:, devices:].T)


def fetch(near_ref, far_ref, held, sems):
    half = near_ref.shape[0]
    copies = [
        pltpu.make_async_copy(near_ref, held.at[pl.ds(0, half)], sems.at[0]),
        pltpu.make_async_copy(far_ref, held.at[pl.ds(half, half)], sems.at[1]),
    ]
    for copy in copies:
        copy.start()
    for copy in copies:
        copy.wait()


def pack_kernel(group, direct, items, send, far, near_ref, far_ref, out_ref, held, gathered, turned, sems):
    step = pl.program_id(0)
    chips = pl.num_programs(0) * group

    @pl.when(step == 0)
    def _():
        fetch(near_ref, far_ref, held, sems)
        if items:
            for q in range(items):
                for p in range(ITEM):
                    gathered[pl.ds(q * ITEM * UNIT + p * UNIT, UNIT), :] = held[far[q * ITEM + p]]
            rows = items * chips
            o = lax.broadcasted_iota(jnp.int32, (128, rows), 0)
            i = lax.broadcasted_iota(jnp.int32, (128, rows), 1)
            for part in range(rows // 128):
                at = o + part * 128
                take = ((at % items) * chips + at // items == i).astype(jnp.float32).astype(jnp.bfloat16)
                turned[pl.ds(part * 128, 128), :] = jnp.dot(
                    take, gathered[...], preferred_element_type=jnp.float32
                ).astype(jnp.bfloat16)

    for k in range(group):
        slot = step * group + k
        for p in range(direct):
            out_ref[k, pl.ds(p * UNIT, UNIT), :] = held[send[p * chips + slot]]
        if items:
            out_ref[k, pl.ds(direct * UNIT, items), :] = turned[pl.ds(pl.multiple_of(slot * items, items), items), :]


def pack(direct, items, send, far, near_units, far_units):
    units, _, depth = near_units.shape
    chips = send.shape[1]
    rows = direct * UNIT + items
    group = 4
    some = max(items, 16)
    return pl.pallas_call(
        functools.partial(pack_kernel, group, direct, items),
        grid_spec=pltpu.PrefetchScalarGridSpec(
            num_scalar_prefetch=2,
            grid=(chips // group,),
            in_specs=[pl.BlockSpec(memory_space=pl.ANY)] * 2,
            out_specs=pl.BlockSpec((group, rows, depth), lambda i, *_: (i, 0, 0)),
            scratch_shapes=[
                pltpu.VMEM((2 * units, UNIT, depth), jnp.bfloat16),
                pltpu.VMEM((some * ITEM * UNIT, depth), jnp.bfloat16),
                pltpu.VMEM((some * chips, depth), jnp.bfloat16),
                pltpu.SemaphoreType.DMA((2,)),
            ],
        ),
        out_shape=jax.ShapeDtypeStruct((chips, rows, depth), jnp.bfloat16),
        compiler_params=pltpu.CompilerParams(vmem_limit_bytes=40 * MIB),
        name="pack",
    )(send.reshape(-1), far.reshape(-1), near_units, far_units)


def score_kernel(group, by_edge, seg, counts, near_ref, far_ref, arrived_ref, back_ref, best_ref, held, row_best, sems):
    step = pl.program_id(0)
    rows = arrived_ref.shape[1]
    width = held.shape[1]
    slots = pl.num_programs(0) * group

    @pl.when(step == 0)
    def _():
        fetch(near_ref, far_ref, held, sems)
        best_ref[...] = jnp.full(best_ref.shape, -1.0, jnp.float32)

    i = lax.broadcasted_iota(jnp.int32, (rows, width), 0)
    j = lax.broadcasted_iota(jnp.int32, (rows, width), 1)
    for k in range(group):
        slot = step * group + k
        row_best[k] = jnp.full((rows, width), -1.0, jnp.float32)

        def segment(e, carry):
            made = seg[e * slots + slot] if by_edge else seg[slot * SHARE + e]

            @pl.when(made > 0)
            def _():
                block = made >> 16
                top = ((made >> 10) & 63) * UNIT
                scores = lax.dot_general(
                    arrived_ref[k], held[block], (((1,), (1,)), ((), ())), preferred_element_type=jnp.float32
                )
                keep = (i >= top) & (i < (made & 1023)) & (j < counts[block])
                scores = jnp.where(keep, scores, -1.0)
                row_best[k] = jnp.maximum(row_best[k], scores)
                best_ref[pl.ds(block, 1), :] = jnp.maximum(
                    best_ref[pl.ds(block, 1), :], jnp.max(scores, axis=0, keepdims=True)
                )

            return carry

        lax.fori_loop(0, SHARE, segment, 0)
        back_ref[pl.ds(k, 1), :] = jnp.max(row_best[k].T, axis=0, keepdims=True)


def score(seg, by_edge, counts, near, far, arrived, rows):
    blocks, width, depth = near.shape
    slots = arrived.shape[0]
    group = 8
    return pl.pallas_call(
        functools.partial(score_kernel, group, by_edge),
        grid_spec=pltpu.PrefetchScalarGridSpec(
            num_scalar_prefetch=2,
            grid=(slots // group,),
            in_specs=[pl.BlockSpec(memory_space=pl.ANY)] * 2
            + [pl.BlockSpec((group, rows, depth), lambda i, *_: (i, 0, 0))],
            out_specs=[
                pl.BlockSpec((group, rows), lambda i, *_: (i, 0)),
                pl.BlockSpec((2 * blocks, width), lambda i, *_: (0, 0)),
            ],
            scratch_shapes=[
                pltpu.VMEM((2 * blocks, width, depth), jnp.bfloat16),
                pltpu.VMEM((group, rows, width), jnp.float32),
                pltpu.SemaphoreType.DMA((2,)),
            ],
        ),
        out_shape=[
            jax.ShapeDtypeStruct((slots, rows), jnp.float32),
            jax.ShapeDtypeStruct((2 * blocks, width), jnp.float32),
        ],
        compiler_params=pltpu.CompilerParams(vmem_limit_bytes=48 * MIB),
        name="score",
    )(seg.reshape(-1), counts, near, far, arrived)


def one_hot(index, count, valid):
    return (index[:, None] == jnp.arange(count, dtype=jnp.int32)[None, :]) & valid[:, None]


def exchange(values, chips):
    groups = [[2 * x + c for x in range(chips)] for c in range(2)]
    return lax.all_to_all(values, "shard", split_axis=0, concat_axis=0, axis_index_groups=groups, tiled=True)


def far_maxima(direct, items, plan, counts, near, far):
    send, own_items, seg, far_seg, hand, target, item_back, _ = plan
    blocks, width, depth = near.shape
    chips = send.shape[1]
    outgoing = pack(
        direct, items, send, own_items,
        near.reshape(-1, UNIT, depth), far.reshape(-1, UNIT, depth),
    )
    arrived = exchange(outgoing, chips)
    rows = direct * UNIT
    if items:
        held = arrived[:, rows:, :].reshape(chips * items, depth)
        take = one_hot(hand.reshape(-1), chips * items, jnp.full((chips * items,), True))
        passed = jnp.dot(take.astype(jnp.bfloat16), held, preferred_element_type=jnp.bfloat16)
        relayed = exchange(passed.reshape(chips, items, depth), chips)
    back, best = score(seg, True, counts, near, far, arrived, rows)
    places = direct
    if items:
        relayed = relayed.swapaxes(0, 1)
        far_back, far_best = score(far_seg, False, counts, near, far, relayed, chips)
        best = jnp.maximum(best, far_best)
        hit = item_back.T[:, :, None] == jnp.arange(items, dtype=jnp.int32)[None, None, :]
        far_back = jnp.where(hit[..., None], far_back[None, None], -1.0).max(axis=2)
        back = jnp.concatenate([back, far_back.reshape(chips, -1)], axis=1)
        places = direct + 8
    returned = exchange(back, chips).reshape(chips, places, UNIT)
    spots = target[:places].T.reshape(-1)
    values = returned.reshape(-1, UNIT).T
    number = 2 * blocks * width // UNIT
    hit = spots[:, None] == jnp.arange(number, dtype=jnp.int32)[None, :]
    folded = jnp.where(hit[None], values[:, :, None], -1.0).max(axis=1)
    return jnp.maximum(best, folded.T.reshape(2 * blocks, width))


def on_device(embeddings, block_rows, pairs):
    blocks = block_rows.shape[0]
    width = embeddings.shape[0] // blocks
    peers = lax.axis_size("shard")
    myself = lax.axis_index("shard")
    swap = [(d, d ^ 1) for d in range(peers)]
    row_block, col_block = pairs[:, 0], pairs[:, 1]
    alive = pairs[:, 2] == myself
    owner = row_block // blocks
    remote = alive & (owner != myself)
    row_local, col_local = row_block % blocks, col_block % blocks
    code = row_local * blocks + col_local
    wanted = jnp.max(jnp.where(one_hot(owner, peers, remote), code[:, None], -1), axis=0)
    tell = jnp.concatenate([wanted, block_rows])[None]
    told = lax.all_to_all(
        jnp.broadcast_to(tell, (peers, tell.shape[1])), "shard", split_axis=0, concat_axis=0, tiled=True
    )

    unit = normalize(embeddings)
    near = unit.reshape(blocks, width, -1)
    far = lax.ppermute(near, "shard", swap)

    nearby = alive & ~remote
    row_table = one_hot(row_local, blocks, nearby).astype(jnp.float32)
    col_table = one_hot(col_local, blocks, nearby).astype(jnp.float32)
    adjacency = (
        lax.dot_general(row_table, col_table, (((0,), (0,)), ((), ())), preferred_element_type=jnp.float32) > 0.5
    )
    best = nearby_maxima(unit, block_rows, adjacency | adjacency.T)

    direct, items = 8, 16
    plan = make_plan(direct, items, told, myself)
    counts = jnp.concatenate([block_rows, lax.dynamic_slice_in_dim(told, myself ^ 1, 1, 0)[0, peers:]])
    near, far, best, plan, counts = lax.optimization_barrier((near, far, best, plan, counts))

    def usual():
        return far_maxima(direct, items, plan, counts, near, far)

    def roomy():
        return far_maxima(16, 0, make_plan(16, 0, told, myself), counts, near, far)

    both = lax.cond(plan[-1][0] > 0, usual, roomy)
    other = lax.ppermute(both[blocks:], "shard", swap)
    return jnp.maximum(best, jnp.maximum(both[:blocks], other))


def solution(mesh):
    placed = (P("shard", None), P("shard"), P("shard", None))
    return jax.shard_map(
        on_device, mesh=mesh, in_specs=placed, out_specs=P("shard", None), check_vma=False
    )
```

time: 664 us -> 390 us (0.59)
  waiting for transfers between devices: 487 us -> 9.06 us
  blocking collectives: 0 us -> 218 us
  Pallas kernels: 72.1 us -> 97.6 us
  matrix products: 22.5 us -> 4.23 us
  between operations: 13.6 us -> 0.81 us
  local copies, waits for them, and re-layouts: 18.9 us -> 12.1 us
    unnamed x2 -> x0, waiting for transfers between devices: 262 us -> none
    all_to_all x0 -> x1, blocking collectives: none -> 218 us  [exchange(): lax.all_to_all(values, 'shard', split_axis=0, concat_axis=0, axis_index_g...]
    all_to_all x3, waiting for transfers between devices: 225 us -> 8.23 us  [the longest x2 8.22 us: exchange(): lax.all_to_all(values, 'shard', split_axis=0, concat_axis=0, axis_index_g...]
    pallas_call x4 -> x5, Pallas kernels: 64.9 us -> 90.4 us  [the longest x2 48.3 us: score(): pl.pallas_call(functools.partial(score_kernel, group, by_edge), grid_spec...]
    dot_general x4 -> x1, matrix products: 21.9 us -> 3.69 us  [far_maxima(): jnp.dot(take.astype(jnp.bfloat16), held, preferred_element_type=jnp.bfloa...]
    broadcast_in_dim x5 -> x1, local copies, waits for them, and re-layouts: 13.9 us -> 0.72 us  [on_device(): jnp.broadcast_to(tell, (peers, tell.shape[1]))]
    cond x0 -> x4, local copies, waits for them, and re-layouts: none -> 7.49 us
  transfers between devices with their start and end apart: 4 -> 5, of which waited for: 3 -> 2; matrix products, arithmetic and copies ran while one was open for 6% -> 1% of each run, Pallas kernels for 5% -> 17%
where the time goes in v2:
time: 390 us; the launch traced here: 389 us
  blocking collectives  218 us (56%)
  Pallas kernels  97.6 us (25%)
  starting transfers between devices  42 us (11%)
  local copies, waits for them, and re-layouts  12.1 us (3%)
  waiting for transfers between devices  9.06 us (2%)
  other arithmetic  4.57 us (1%)
  matrix products  4.23 us (1%)
    all_to_all x1, blocking collectives, exchange(): lax.all_to_all(values, 'shard', split_axis=0, concat_axis=0, axis_index_g...  218 us
    pallas_call x2, Pallas kernels, score(): pl.pallas_call(functools.partial(score_kernel, group, by_edge), grid_spec...  48.3 us
    all_to_all x2, starting transfers between devices, exchange(): lax.all_to_all(values, 'shard', split_axis=0, concat_axis=0, axis_index_g...  26.2 us
    pallas_call x1, Pallas kernels, nearby_maxima(): pl.pallas_call(nearby_kernel, grid_spec=pltpu.PrefetchScalarGridSpec(num_...  16.5 us
    pallas_call x1, Pallas kernels, pack(): pl.pallas_call(functools.partial(pack_kernel, group, direct, items), grid...  15.8 us
    all_to_all x1, starting transfers between devices, on_device(): lax.all_to_all(jnp.broadcast_to(tell, (peers, tell.shape[1])), 'shard', s...  10.2 us
    pallas_call x1, Pallas kernels, make_plan(): pl.pallas_call(functools.partial(plan_kernel, direct, items, chips), in_s...  9.8 us
    all_to_all x2, waiting for transfers between devices, exchange(): lax.all_to_all(values, 'shard', split_axis=0, concat_axis=0, axis_index_g...  8.22 us
  transfers between devices with their start and end apart: 5, of which 2 were waited for; matrix products, arithmetic and copies ran while one was open for 1% of the time, Pallas kernels for 17%

profile of v2, /device:TPU:1, one launch (start us, length us, event | category | flops | bytes accessed | tf_op | source)
XLA Modules:
  0.0 388.6 jit_solution(6320314828141469475)
XLA Ops:
  0.0 7.2 %normalize.1.unit_ref = bf16[2048,1024]{1,0:T(8,128)(2,1)} custom-call(bf16[2048,1024]{1,0:T(8,128)(2,1)} %values_ref.1), custom_call_target="tpu_custom_call" | custom-call | tf_op jit(solution)/shard_map/normalize/pallas_call | solution.py:26
  7.3 1.4 collective-permute-start
  8.8 0.3 select_reduce_fusion.3
  9.1 0.7 broadcast_in_dim.97
  9.8 10.2 %all-to-all-start.5 = ((s32[128,1,144]{2,1,0:T(1,128)}), s32[128,1,144]{2,1,0:T(1,128)S(1)}, u32[]{:S(2)}, u32[]{:S(2)}) async-start(s32[128,1,144]{2,1,0:T(1,128)} %broadcast_in_dim.97), calls=%async_computation.5 | async-start | bytes 262144 | tf_op jit(solution)/shard_map/all_to_all | solution.py:534
  20.0 0.5 convolution_compare_fusion
  20.7 16.5 %nearby.1 = f32[16,128]{1,0:T(8,128)S(1)} custom-call(s32[36]{0:T(128)S(1)} %copy-done.1, s32[36]{0:T(128)S(1)} %copy-done.2, s32[256]{0:T(256)S(1)} %reshape.166.linked, s32[16]{0:T(128)S(1)} %copy-done, bf16[2048,1024]{1,0:T(8,128)(2,1)} %normalize.1.unit_ref), custom_call_target="tpu_custom_call" | custom-call | tf_op jit(solution)/shard_map/nearby/pallas_call | solution.py:74
  37.6 9.8 %plan.3 = (s32[8,64]{1,0:T(8,128)S(1)}, s32[16,4]{1,0:T(8,128)S(1)}, s32[8,64]{1,0:T(8,128)S(1)}, s32[16,8]{1,0:T(8,128)S(1)}, s32[64,16]{1,0:T(8,128)S(1)}, /*i...) custom-call(s32[1]{0:T(128)} %bitcast.23.me_ref, s32[128,128]{1,0:T(8,128)S(1)} %copy.52.pair_ref, ...), custom_call_target="tpu_custom_call" | custom-call | tf_op jit(solution)/shard_map/plan/pallas_call | solution.py:315
  48.2 334.8 %conditional.1 = (f32[32,128]{1,0:T(8,128)S(1)}, f32[32,128]{1,0:T(8,128)S(1)}) conditional(s32[]{:T(128)} %bitcast.30, (s32[]{:T(128)}, s32[128,144]{0,1:T(8,128)S(1)}, bf16[16,128,1024]{2,1,0:T(8,128)(2,1)}, bf16[16,128,1024]{2,1,0:T(8,128)(2,1)}, s32[32]{0:T(128)S(1)}) %tuple.36, (s32[8,64]{1,0:T(8,128)S(1)}, s32[8,64]{1,0:T(8,128)S(1)}, ...), branch_computations={%region_1.3_spmd, %region_3.6_spmd} | conditional | flops 2157455360 | bytes 150613136 | solution.py:561
  48.5 15.8 %pack.3 = bf16[64,144,1024]{2,1,0:T(8,128)(2,1)} custom-call(s32[512]{0:T(512)S(1)} %reshape.148.send, s32[64]{0:T(128)S(1)} %reshape.149.far, bf16[128,16,1024]{2,1,0:T(8,128)(2,1)} %bitcast.52, bf16[128,16,1024]{2,1,0:T(8,128)(2,1)} %bitcast.9.far_ref), custom_call_target="tpu_custom_call" | custom-call | tf_op jit(solution)/shard_map/cond/branch_1_fun/pack/pallas_call | solution.py:387
  64.3 217.9 %all_to_all.35.arrived_ref = bf16[64,144,1024]{2,1,0:T(8,128)(2,1)S(1)} all-to-all(bf16[64,144,1024]{2,1,0:T(8,128)(2,1)} %pack.3), channel_id=1, replica_groups={{0,2,4,6,8,10,12,14,16,18,20,22,24,26,28,30,32,34,36,38,40,42,44,46,48,..., dimensions={0} | all-to-all | bytes 37748736 | tf_op jit(solution)/shard_map/cond/branch_1_fun/all_to_all | solution.py:483
  282.2 6.5 %copy-done.4 = bf16[64,144,1024]{2,1,0:T(8,128)(2,1)} copy-done((bf16[64,144,1024]{2,1,0:T(8,128)(2,1)}, bf16[64,144,1024]{2,1,0:T(8,128)(2,1)S(1)}, u32[]{:S(2)}) %copy-start.4) | copy-done | bytes 18874392 | tf_op jit(solution)/shard_map/cond
  288.7 0.3 slice.47
  289.0 3.7 fusion.1
  292.7 16.3 %all-to-all-start.3 = ((bf16[64,16,1024]{2,1,0:T(8,128)(2,1)}), bf16[64,16,1024]{2,1,0:T(8,128)(2,1)S(1)}, u32[]{:S(2)}, u32[]{:S(2)}) async-start(bf16[64,16,1024]{2,1,0:T(8,128)(2,1)} %fusion.1), calls=%async_computation.3 | async-start | bytes 4194304 | tf_op jit(solution)/shard_map/cond/branch_1_fun/all_to_all | solution.py:483
  309.3 0.1 iota_compare_fusion.3
  309.5 39.7 %score.4 = (f32[64,128]{1,0:T(8,128)S(1)}, f32[32,128]{1,0:T(8,128)S(1)}) custom-call(s32[512]{0:T(512)S(1)} %reshape.147.seg, s32[32]{0:T(128)S(1)} %get-tuple-element.51.counts, bf16[16,128,1024]{2,1,0:T(8,128)(2,1)} %get-tuple-element.52.near_ref, bf16[16,128,1024]{2,1,0:T(8,128)(2,1)} %get-tuple-element.53.far_ref, bf16[64,144,1024]{2,1,0:T(8,128)(2,1)} %copy-done.4), custom_call_target="tpu_custom_call" | custom-call | tf_op jit(solution)/shard_map/cond/branch_1_fun/score/pallas_call | solution.py:451
  349.2 1.2 copy.57
  350.4 1.0 copy-done.3
  351.4 8.6 %score.5 = (f32[16,64]{1,0:T(8,128)S(1)}, f32[32,128]{1,0:T(8,128)S(1)}) custom-call(s32[128]{0:T(128)S(1)} %reshape.152.seg, s32[32]{0:T(128)S(1)} %get-tuple-element.51.counts, bf16[16,128,1024]{2,1,0:T(8,128)(2,1)S(1)} %copy-done.3, bf16[16,128,1024]{2,1,0:T(8,128)(2,1)} %get-tuple-element.53.far_ref, bf16[16,64,1024]{2,1,0:T(8,128)(2,1)S(1)} %bitcast.46), custom_call_target="tpu_custom_call" | custom-call | tf_op jit(solution)/shard_map/cond/branch_1_fun/score/pallas_call | solution.py:451
  360.0 0.4 select_reduce_fusion.2
  360.5 0.7 copy.47
  361.2 10.0 %all-to-all-start.4 = ((f32[64,1,256]{2,1,0:T(1,128)}), f32[64,1,256]{2,1,0:T(1,128)S(1)}, u32[]{:S(2)}, u32[]{:S(2)}) async-start(f32[64,1,256]{2,1,0:T(1,128)} %copy.47), calls=%async_computation.4 | async-start | bytes 131072 | tf_op jit(solution)/shard_map/cond/branch_1_fun/all_to_all | solution.py:483
  371.2 0.2 iota_compare_fusion.2
  371.4 8.2 %all-to-all-done.4 = f32[64,1,256]{2,1,0:T(1,128)S(1)} async-done(((f32[64,1,256]{2,1,0:T(1,128)}), f32[64,1,256]{2,1,0:T(1,128)S(1)}, u32[]{:S(2)}, u32[]{:S(2)}) %all-to-all-start.4) | async-done | bytes 65568 | tf_op jit(solution)/shard_map/cond/branch_1_fun/all_to_all | solution.py:483
  379.7 0.2 reduce.1
  379.8 0.2 reshape.155
  380.0 0.2 copy.48
  380.2 2.6 select_reduce_fusion.1
  383.0 4.2 %collective-permute-start.1 = (f32[16,128]{1,0:T(8,128)S(1)}, f32[16,128]{1,0:T(8,128)S(1)}, u32[]{:S(2)}, u32[]{:S(2)}) collective-permute-start(f32[16,128]{1,0:T(8,128)S(1)} %slice.52), channel_id=1, source_target_pairs={{0,1},{1,0},{2,3},{3,2},{4,5},{5,4},{6,7},{7,6},{8,9},{9,8},{10,11... | collective-permute-start | bytes 24584 | tf_op jit(solution)/shard_map/ppermute | solution.py:562
  387.2 0.8 collective-permute-done.1
  388.0 0.6 fusion.12
  (42 shorter events, 1.6 us)
Async XLA Ops:
  0.0 20.7 %copy-start.1 = (s32[36]{0:T(128)S(1)}, s32[36]{0:T(128)}, u32[]{:S(2)}) copy-start(s32[36]{0:T(128)} %constant.62.clone.first) | copy-start | bytes 436
  0.0 20.7 %copy-start.2 = (s32[36]{0:T(128)S(1)}, s32[36]{0:T(128)}, u32[]{:S(2)}) copy-start(s32[36]{0:T(128)} %constant.63.clone.second) | copy-start | bytes 436
  0.0 8.7 %copy-start.5 = (s32[512,3]{0,1:T(4,128)S(1)}, s32[512,3]{0,1:T(4,128)}, u32[]{:S(2)}) copy-start(s32[512,3]{0,1:T(4,128)} %param.9) | copy-start | bytes 18436
  0.0 9.0 %copy-start = (s32[16]{0:T(128)S(1)}, s32[16]{0:T(128)}, u32[]{:S(2)}) copy-start(s32[16]{0:T(128)} %counts.1) | copy-start | bytes 196
  7.3 40.2 %collective-permute-start = (bf16[16,128,1024]{2,1,0:T(8,128)(2,1)}, bf16[16,128,1024]{2,1,0:T(8,128)(2,1)}, u32[]{:S(2)}, u32[]{:S(2)}) collective-permute-start(bf16[16,128,1024]{2,1,0:T(8,128)(2,1)} %bitcast.48), channel_id=1, source_target_pairs={{0,1},{1,0},{2,3},{3,2},{4,5},{5,4},{6,7},{7,6},{8,9},{9,8},{10,11... | collective-permute-start | bytes 12582920 | tf_op jit(solution)/shard_map/ppermute | solution.py:540
  9.8 27.5 %all-to-all-start.5 = ((s32[128,1,144]{2,1,0:T(1,128)}), s32[128,1,144]{2,1,0:T(1,128)S(1)}, u32[]{:S(2)}, u32[]{:S(2)}) async-start(s32[128,1,144]{2,1,0:T(1,128)} %broadcast_in_dim.97), calls=%async_computation.5 | async-start | bytes 262144 | tf_op jit(solution)/shard_map/all_to_all | solution.py:534
  282.2 6.5 %copy-start.4 = (bf16[64,144,1024]{2,1,0:T(8,128)(2,1)}, bf16[64,144,1024]{2,1,0:T(8,128)(2,1)S(1)}, u32[]{:S(2)}) copy-start(bf16[64,144,1024]{2,1,0:T(8,128)(2,1)S(1)} %all_to_all.35.arrived_ref) | copy-start | bytes 56623108 | tf_op jit(solution)/shard_map/cond
  292.7 56.5 %all-to-all-start.3 = ((bf16[64,16,1024]{2,1,0:T(8,128)(2,1)}), bf16[64,16,1024]{2,1,0:T(8,128)(2,1)S(1)}, u32[]{:S(2)}, u32[]{:S(2)}) async-start(bf16[64,16,1024]{2,1,0:T(8,128)(2,1)} %fusion.1), calls=%async_computation.3 | async-start | bytes 4194304 | tf_op jit(solution)/shard_map/cond/branch_1_fun/all_to_all | solution.py:483
  349.2 2.2 copy-start.3
  361.2 18.4 %all-to-all-start.4 = ((f32[64,1,256]{2,1,0:T(1,128)}), f32[64,1,256]{2,1,0:T(1,128)S(1)}, u32[]{:S(2)}, u32[]{:S(2)}) async-start(f32[64,1,256]{2,1,0:T(1,128)} %copy.47), calls=%async_computation.4 | async-start | bytes 131072 | tf_op jit(solution)/shard_map/cond/branch_1_fun/all_to_all | solution.py:483
  383.0 5.0 %collective-permute-start.1 = (f32[16,128]{1,0:T(8,128)S(1)}, f32[16,128]{1,0:T(8,128)S(1)}, u32[]{:S(2)}, u32[]{:S(2)}) collective-permute-start(f32[16,128]{1,0:T(8,128)S(1)} %slice.52), channel_id=1, source_target_pairs={{0,1},{1,0},{2,3},{3,2},{4,5},{5,4},{6,7},{7,6},{8,9},{9,8},{10,11... | collective-permute-start | bytes 24584 | tf_op jit(solution)/shard_map/ppermute | solution.py:562
